TPU v7x, 32 devices: a whole 2x2x4 slice. The times are simulated.
32 devices in a mesh: rows: 4 (over y, core), cols: 8 (over z, x).
Axes of the slice: x: 2, y: 2, z: 4, core: 2. Of those that a mesh axis runs over, the one named last changes fastest.
Arguments:
- band_input: bfloat16 [256, 256, 512], P('rows', 'cols'), may hold values from -1000 to 1000
- column_taps: float32 [21, 512], replicated, may hold values from -1 to 1
- row_taps: float32 [21, 512], replicated, may hold values from -1 to 1
- w_squeeze: bfloat16 [512, 512], replicated, may hold values from -0.25 to 0.25
- bases_init: float32 [512, 64], replicated, may hold values from 0.004 to 0.12
- w_ham: bfloat16 [512, 512], replicated, may hold values from -0.25 to 0.25
- w_align: bfloat16 [512, 512], replicated, may hold values from -0.25 to 0.25
Outputs:
- head_out: bfloat16 [256, 256, 512], P('rows', 'cols')
All inputs are finite; a program needn't handle non-finite values.
Results may differ from a plain program's by a relative error of at most 0.0071.
The roundings to bfloat16 on the way count: a program that leaves them out, or rounds other values in their place, can miss the bound.
Values may be sent and summed in bfloat16 or wider, within the bound.
A program may use at most 64 MiB of HBM per device.

v0:
```python
import jax
import jax.numpy as jnp
from jax import lax
from jax.sharding import PartitionSpec as P

STEPS = 3


EPS = 1e-06


def padded(x, sides, width):
    for axis, dim in sides:
        count, length = (lax.axis_size(axis), x.shape[dim])
        up = [(i, (i + 1) % count) for i in range(count - 1)]
        down = [(j, i) for i, j in up]
        last = lax.slice_in_dim(x, length - width, length, axis=dim)
        initial = lax.slice_in_dim(x, 0, width, axis=dim)
        before = lax.ppermute(last, axis, up)
        after = lax.ppermute(initial, axis, down)
        x = jnp.concatenate([before, x, after], axis=dim)
    return x


def filter_columns(widened, column_taps, extent):
    summed = jnp.zeros((widened.shape[0], extent, widened.shape[2]), jnp.float32)
    for offset in range(column_taps.shape[0]):
        summed = summed + column_taps[offset] * widened[:, offset : offset + extent, :].astype(
            jnp.float32
        )
    return summed


def filter_rows(extended, row_taps, extent):
    summed = jnp.zeros((extent, extended.shape[1], extended.shape[2]), jnp.float32)
    for offset in range(row_taps.shape[0]):
        summed = summed + row_taps[offset] * extended[offset : offset + extent].astype(jnp.float32)
    return summed


def update_coeffs(feature, basis_now, coeffs):
    numerator = lax.dot_general(
        basis_now.astype(jnp.bfloat16),
        feature,
        (((0,), (1,)), ((), ())),
        preferred_element_type=jnp.float32,
    )
    gram_local = jnp.dot(basis_now.T, basis_now, precision=lax.Precision.HIGHEST)
    denominator = jnp.dot(gram_local, coeffs, precision=lax.Precision.HIGHEST)
    return coeffs * numerator / (denominator + EPS)


def on_device(band_input, column_taps, row_taps, w_squeeze, bases_init, w_ham, w_align):
    tile_rows, tile_cols, channels = band_input.shape
    margin = column_taps.shape[0] // 2
    widened = padded(band_input, (("cols", 1),), margin)
    col_filtered = filter_columns(widened, column_taps, tile_cols).astype(jnp.bfloat16)
    extended = padded(col_filtered, (("rows", 0),), margin)
    strip_sum = filter_rows(extended, row_taps, tile_rows)
    mixed_tile = (
        (band_input.astype(jnp.float32) + strip_sum)
        .astype(jnp.bfloat16)
        .reshape(tile_rows * tile_cols, channels)
    )
    feature = jax.nn.relu(
        jnp.dot(mixed_tile, w_squeeze, preferred_element_type=jnp.float32)
    ).astype(jnp.bfloat16)
    basis_now = bases_init
    scores = lax.dot_general(
        basis_now.astype(jnp.bfloat16),
        feature,
        (((0,), (1,)), ((), ())),
        preferred_element_type=jnp.float32,
    )
    coeffs = jax.nn.softmax(scores, axis=0)
    for iteration in range(STEPS):
        coeffs = update_coeffs(feature, basis_now, coeffs)
        coeff_low = coeffs.astype(jnp.bfloat16)
        numerator = lax.dot_general(
            feature, coeff_low, (((0,), (1,)), ((), ())), preferred_element_type=jnp.float32
        )
        gram_part = jnp.dot(coeffs, coeffs.T, precision=lax.Precision.HIGHEST)
        numerator, gram_sum = lax.psum((numerator, gram_part), ("rows", "cols"))
        basis_now = (
            basis_now
            * numerator
            / (jnp.dot(basis_now, gram_sum, precision=lax.Precision.HIGHEST) + EPS)
        )
    coeffs = update_coeffs(feature, basis_now, coeffs)
    rebuilt = lax.dot_general(
        coeffs.astype(jnp.bfloat16),
        basis_now.astype(jnp.bfloat16),
        (((0,), (1,)), ((), ())),
        preferred_element_type=jnp.float32,
    ).astype(jnp.bfloat16)
    ham_term = jnp.dot(rebuilt, w_ham, preferred_element_type=jnp.float32)
    hammed = jax.nn.relu(feature.astype(jnp.float32) + ham_term).astype(jnp.bfloat16)
    head_out = jnp.dot(hammed, w_align, preferred_element_type=jnp.float32).astype(jnp.bfloat16)
    return head_out.reshape(tile_rows, tile_cols, channels)


def solution(mesh):
    in_specs = (P("rows", "cols", None), P(), P(), P(), P(), P(), P())
    out_specs = P("rows", "cols", None)
    return jax.shard_map(
        on_device, mesh=mesh, in_specs=in_specs, out_specs=out_specs, check_vma=False
    )
```

profile of v0, /device:TPU:0, one launch (start us, length us, event | category | flops | bytes accessed | tf_op | source)
XLA Modules:
  0.0 482.9 jit_solution(7527231827866830900)
XLA Ops:
  6.5 2.1 fusion.69
  9.1 5.0 %collective-permute-start = (bf16[64,10,512]{2,0,1:T(8,128)(2,1)S(1)}, bf16[64,10,512]{2,0,1:T(8,128)(2,1)S(1)}, u32[]{:S(2)}, u32[]{:S(2)}) collective-permute-start(bf16[64,10,512]{2,0,1:T(8,128)(2,1)S(1)} %copy.12), channel_id=1, source_target_pairs={{0,1},{1,2},{2,3},{3,4},{4,5},{5,6},{6,7},{8,9},{9,10},{10,11},{11... | collective-permute-start | bytes 1966088 | tf_op jit(solution)/shard_map/ppermute | solution.py:19
  14.5 1.3 collective-permute-start.1
  16.1 26.0 %collective-permute-done = bf16[64,10,512]{2,0,1:T(8,128)(2,1)S(1)} collective-permute-done((bf16[64,10,512]{2,0,1:T(8,128)(2,1)S(1)}, bf16[64,10,512]{2,0,1:T(8,128)(2,1)S(1)}, u32[]{:S(2)}, u32[]{:S(2)}) %collective-permute-start) | collective-permute-done | bytes 655392 | tf_op jit(solution)/shard_map/ppermute | solution.py:19
  42.9 13.5 %fusion.11 = bf16[64,32,512]{2,1,0:T(8,128)(2,1)S(1)} fusion(bf16[64,32,512]{2,1,0:T(8,128)(2,1)S(1)} %copy-done.1, bf16[64,10,512]{2,1,0:T(8,128)(2,1)S(1)} %copy.9, bf16[64,42,512]{2,1,0:T(8,128)(2,1)S(1)} %copy_dynamic-update-slice_fusion, f32[512]{0:T(512)S(1)} %bitcast.145, f32[512]{0:T(512)S(1)} %bitcast.144, f32[512]{0:T(512)S(1)} %bitcast.126, ...), kind=kLoop, calls=%fused_computation.49 | loop fusion | flops 97517568 | bytes 25864192 | tf_op jit(solution)/shard_map/convert_element_type | solution.py:57
  56.5 1.3 collective-permute-start.3
  57.8 3.1 collective-permute-start.2
  62.0 14.4 %fusion.12 = bf16[64,32,512]{2,1,0:T(8,128)(2,1)S(1)} fusion(bf16[64,32,512]{2,1,0:T(8,128)(2,1)S(1)} %copy-done.1, bf16[64,32,512]{2,1,0:T(8,128)(2,1)S(1)} %fusion.11, bf16[10,32,512]{2,1,0:T(8,128)(2,1)S(1)} %collective-permute-done.3, bf16[10,32,512]{2,1,0:T(8,128)(2,1)S(1)} %collective-permute-done.2, f32[512]{0:T(512)S(1)} %bitcast.124, ...), kind=kLoop, calls=%fused_computation.50 | loop fusion | flops 89128960 | bytes 6989824 | tf_op jit(solution)/shard_map/convert_element_type | solution.py:62
  76.4 1.2 maximum_convert_fusion.1
  81.0 46.4 %psum.43 = f32[64,64]{1,0:T(8,128)S(1)} all-reduce(f32[64,64]{1,0:T(8,128)S(1)} %fusion.76), channel_id=1, replica_groups=mesh['rows'=4,'cols'=8] {'rows','cols'}, use_global_device_ids=true, to_apply=%region_3.4 | all-reduce | flops 4096 | bytes 32768 | tf_op jit(solution)/shard_map/psum | solution.py:83
  127.4 82.3 %all-reduce.4.cloned.1.call-done = f32[512,64]{0,1:T(8,128)} async-done(((f32[512,64]{0,1:T(8,128)}), f32[512,64]{0,1:T(8,128)}) %all-reduce.4.cloned.1.call-update) | async-done | bytes 131088 | tf_op jit(solution)/shard_map/psum | solution.py:83
  209.7 1.2 fusion.46
  212.0 1.4 fusion.15
  213.4 2.2 fusion.55
  215.6 1.8 fusion.78
  217.4 39.5 %psum.45 = f32[64,64]{1,0:T(8,128)S(1)} all-reduce(f32[64,64]{1,0:T(8,128)S(1)} %fusion.78), channel_id=1, replica_groups=mesh['rows'=4,'cols'=8] {'rows','cols'}, use_global_device_ids=true, to_apply=%region_5.6 | all-reduce | flops 4096 | bytes 32768 | tf_op jit(solution)/shard_map/psum | solution.py:83
  257.0 80.3 %all-reduce.6.cloned.1.call-done = f32[512,64]{0,1:T(8,128)} async-done(((f32[512,64]{0,1:T(8,128)}), f32[512,64]{0,1:T(8,128)}) %all-reduce.6.cloned.1.call-update) | async-done | bytes 131088 | tf_op jit(solution)/shard_map/psum | solution.py:83
  337.3 1.2 fusion.47
  338.5 1.8 convolution_multiply_fusion.1
  340.6 1.6 fusion.14
  343.9 39.4 %psum.47 = f32[64,64]{1,0:T(8,128)S(1)} all-reduce(f32[64,64]{1,0:T(8,128)S(1)} %fusion.80), channel_id=1, replica_groups=mesh['rows'=4,'cols'=8] {'rows','cols'}, use_global_device_ids=true, to_apply=%region_7.8 | all-reduce | flops 4096 | bytes 32768 | tf_op jit(solution)/shard_map/psum | solution.py:83
  383.3 81.7 %all-reduce.8.cloned.1.call-done = f32[512,64]{0,1:T(8,128)} async-done(((f32[512,64]{0,1:T(8,128)}), f32[512,64]{0,1:T(8,128)}) %all-reduce.8.cloned.1.call-update) | async-done | bytes 131088 | tf_op jit(solution)/shard_map/psum | solution.py:83
  467.9 4.3 maximum_convert_fusion
  472.2 4.2 convolution_convert_fusion
  (46 shorter events, 12.2 us)
Async XLA Ops:
  6.5 69.9 %copy-start = (bf16[512,512]{1,0:T(8,128)(2,1)S(1)}, bf16[512,512]{1,0:T(8,128)(2,1)}, u32[]{:S(2)}) copy-start(bf16[512,512]{1,0:T(8,128)(2,1)} %param.10) | copy-start | bytes 1572868
  6.5 9.2 %copy-start.1 = (bf16[64,32,512]{2,1,0:T(8,128)(2,1)S(1)}, bf16[64,32,512]{2,1,0:T(8,128)(2,1)}, u32[]{:S(2)}) copy-start(bf16[64,32,512]{2,1,0:T(8,128)(2,1)} %param.7) | copy-start | bytes 6291460
  6.5 203.2 %all-reduce.4.cloned.1.call-start = ((), (), s32[]{:S(2)}) async-start(), calls=%async_computation | async-start | bytes 262144 | tf_op jit(solution)/shard_map/psum | solution.py:83
  9.1 6.9 %copy-start.3 = (f32[21,512]{1,0:T(8,128)S(1)}, f32[21,512]{1,0:T(8,128)}, u32[]{:S(2)}) copy-start(f32[21,512]{1,0:T(8,128)} %param.8) | copy-start | bytes 129028
  9.1 7.0 %copy-start.4 = (f32[21,512]{1,0:T(8,128)S(1)}, f32[21,512]{1,0:T(8,128)}, u32[]{:S(2)}) copy-start(f32[21,512]{1,0:T(8,128)} %param.9) | copy-start | bytes 129028
  9.1 33.0 %collective-permute-start = (bf16[64,10,512]{2,0,1:T(8,128)(2,1)S(1)}, bf16[64,10,512]{2,0,1:T(8,128)(2,1)S(1)}, u32[]{:S(2)}, u32[]{:S(2)}) collective-permute-start(bf16[64,10,512]{2,0,1:T(8,128)(2,1)S(1)} %copy.12), channel_id=1, source_target_pairs={{0,1},{1,2},{2,3},{3,4},{4,5},{5,6},{6,7},{8,9},{9,10},{10,11},{11... | collective-permute-start | bytes 1966088 | tf_op jit(solution)/shard_map/ppermute | solution.py:19
  14.5 28.0 %collective-permute-start.1 = (bf16[64,10,512]{2,0,1:T(8,128)(2,1)S(1)}, bf16[64,10,512]{2,0,1:T(8,128)(2,1)S(1)}, u32[]{:S(2)}, u32[]{:S(2)}) collective-permute-start(bf16[64,10,512]{2,0,1:T(8,128)(2,1)S(1)} %copy.13), channel_id=1, source_target_pairs={{1,0},{2,1},{3,2},{4,3},{5,4},{6,5},{7,6},{9,8},{10,9},{11,10},{12... | collective-permute-start | bytes 1966088 | tf_op jit(solution)/shard_map/ppermute | solution.py:20
  42.9 17.9 %copy-start.2 = (f32[512,64]{0,1:T(8,128)S(1)}, f32[512,64]{0,1:T(8,128)}, u32[]{:S(2)}) copy-start(f32[512,64]{0,1:T(8,128)} %param.11) | copy-start | bytes 393220
  56.5 4.6 collective-permute-start.3
  57.8 4.3 collective-permute-start.2
  80.4 256.9 %all-reduce.6.cloned.1.call-start = ((), (), s32[]{:S(2)}) async-start(), calls=%async_computation.1 | async-start | bytes 262144 | tf_op jit(solution)/shard_map/psum | solution.py:83
  215.6 249.5 %all-reduce.8.cloned.1.call-start = ((), (), s32[]{:S(2)}) async-start(), calls=%async_computation.2 | async-start | bytes 262144 | tf_op jit(solution)/shard_map/psum | solution.py:83
  467.9 4.3 copy-start.5
Sparse Core Ops, SparseCore 0:
  80.5 129.1 all-reduce.3
  215.7 121.5 all-reduce.5
  343.5 121.5 all-reduce.7
where the time goes:
time: 484 us; the launch traced here: 483 us
  waiting for transfers between devices  271 us (56%)
  blocking collectives  125 us (26%)
  matrix products  30.2 us (6%)
  other arithmetic  27.9 us (6%)
  between operations  13.5 us (3%)
  starting transfers between devices  10.7 us (2%)
    psum x3, waiting for transfers between devices, on_device(): numerator, gram_sum = lax.psum((numerator, gram_part), ('rows', 'cols'))  244 us
    psum x3, blocking collectives, on_device(): numerator, gram_sum = lax.psum((numerator, gram_part), ('rows', 'cols'))  125 us
    ppermute x2, waiting for transfers between devices, padded(): before = lax.ppermute(last, axis, up)  26.9 us
    convert_element_type x1, other arithmetic, on_device(): mixed_tile = (band_input.astype(jnp.float32) + strip_sum).astype(jnp.bflo...  14.4 us
    convert_element_type x1, other arithmetic, on_device(): filter_columns(widened, column_taps, tile_cols).astype(jnp.bfloat16)  13.5 us
  transfers between devices with their start and end apart: 7, of which 5 were waited for; matrix products, arithmetic and copies ran while one was open for 1% of the time, Pallas kernels for 0%

commit v1 on v0

v1 whole, which is shorter than its diff:
```python
import functools

import jax
import jax.numpy as jnp
from jax import lax
from jax.experimental import pallas as pl
from jax.experimental.pallas import tpu as pltpu
from jax.sharding import PartitionSpec as P

STEPS = 3


EPS = 1e-06

MESH = pl.DeviceIdType.MESH
HIGHEST = lax.Precision.HIGHEST
NT = (((1,), (1,)), ((), ()))


def padded(x, sides, width):
    for axis, dim in sides:
        count, length = (lax.axis_size(axis), x.shape[dim])
        up = [(i, (i + 1) % count) for i in range(count - 1)]
        down = [(j, i) for i, j in up]
        last = lax.slice_in_dim(x, length - width, length, axis=dim)
        initial = lax.slice_in_dim(x, 0, width, axis=dim)
        before = lax.ppermute(last, axis, up)
        after = lax.ppermute(initial, axis, down)
        x = jnp.concatenate([before, x, after], axis=dim)
    return x


def filter_columns(widened, column_taps, extent):
    summed = jnp.zeros((widened.shape[0], extent, widened.shape[2]), jnp.float32)
    for offset in range(column_taps.shape[0]):
        summed = summed + column_taps[offset] * widened[:, offset : offset + extent, :].astype(
            jnp.float32
        )
    return summed


def filter_rows(extended, row_taps, extent):
    summed = jnp.zeros((extent, extended.shape[1], extended.shape[2]), jnp.float32)
    for offset in range(row_taps.shape[0]):
        summed = summed + row_taps[offset] * extended[offset : offset + extent].astype(jnp.float32)
    return summed


def dot32(a, b):
    return jnp.dot(a, b, preferred_element_type=jnp.float32)


def factor_kernel(
    grid_shape, mixed, w_squeeze, bases, w_ham, w_align, out,
    feature, coeffs, basis_now, part, arrived, line_out, line_in, gathered,
    a_send, a_recv, b_send, b_recv, c_send, c_recv,
):
    n_rows, n_cols, pair, piece = grid_shape
    group, line = n_rows * pair, n_cols // pair
    pixels, channels = mixed.shape
    rank = bases.shape[0]
    depth = rank // group
    blocks = pixels // piece

    row, col = lax.axis_index("rows"), lax.axis_index("cols")
    cell, along = lax.rem(col, pair), lax.div(col, pair)
    member = row * pair + cell

    def in_group(step):
        other = lax.rem(member + step, group)
        return other, (lax.div(other, pair), along * pair + lax.rem(other, pair))

    def in_line(step):
        return (row, lax.rem(along + step, line) * pair + cell)

    barrier = pltpu.get_barrier_semaphore()
    for step in range(1, group):
        pl.semaphore_signal(barrier, inc=1, device_id=in_group(step)[1], device_id_type=MESH)
    for step in range(1, line):
        pl.semaphore_signal(barrier, inc=1, device_id=in_line(step), device_id_type=MESH)

    def copy_a(it, step):
        other, device = in_group(step)
        return pltpu.make_async_remote_copy(
            src_ref=part.at[it, other], dst_ref=arrived.at[it, step],
            send_sem=a_send.at[it, step], recv_sem=a_recv.at[it, step],
            device_id=device, device_id_type=MESH,
        )

    def copy_b(it, step):
        return pltpu.make_async_remote_copy(
            src_ref=line_out.at[it], dst_ref=line_in.at[it, step],
            send_sem=b_send.at[it, step], recv_sem=b_recv.at[it, step],
            device_id=in_line(step), device_id_type=MESH,
        )

    def copy_c(it, step, slot):
        return pltpu.make_async_remote_copy(
            src_ref=gathered.at[it, slot], dst_ref=gathered.at[it, slot],
            send_sem=c_send.at[it, step], recv_sem=c_recv.at[it, step],
            device_id=in_group(step)[1], device_id_type=MESH,
        )

    def reduce_all(it, numerator, gram):
        both = jnp.concatenate([numerator, gram, jnp.zeros_like(gram)], axis=1)
        for index in range(group):
            part[it, index] = both[index * depth : (index + 1) * depth]
        if it == 0:
            pl.semaphore_wait(barrier, group - 1 + line - 1)
        for step in range(1, group):
            copy_a(it, step).start()
        total = part[it, member]
        for step in range(1, group):
            copy_a(it, step).wait_recv()
            total = total + arrived[it, step]
        if line > 1:
            line_out[it] = total
            for step in range(1, line):
                copy_b(it, step).start()
            for step in range(1, line):
                copy_b(it, step).wait_recv()
                total = total + line_in[it, step]
        gathered[it, member] = total
        for step in range(1, group):
            copy_c(it, step, member).start()
        for step in range(1, group):
            copy_c(it, step, lax.rem(member + group - step, group)).wait_recv()
        whole = jnp.concatenate([gathered[it, index] for index in range(group)], axis=0)
        return whole[:, :channels], whole[:, channels : channels + rank]

    def sums(it):
        basis = basis_now[...]
        basis_low = basis.astype(jnp.bfloat16)
        gram_local = lax.dot_general(
            basis, basis, NT, precision=HIGHEST, preferred_element_type=jnp.float32
        )

        def body(index, carry):
            numerator, gram = carry
            span = pl.ds(pl.multiple_of(index * piece, piece), piece)
            if it == 0:
                f = jnp.maximum(dot32(mixed[span, :], w_squeeze[...]), 0.0).astype(jnp.bfloat16)
                feature[span, :] = f
            else:
                f = feature[span, :]
            top = lax.dot_general(basis_low, f, NT, preferred_element_type=jnp.float32)
            if it == 0:
                weight = jnp.exp(top - jnp.max(top, axis=0, keepdims=True))
                now = weight / jnp.sum(weight, axis=0, keepdims=True)
            else:
                now = coeffs[index]
            below = jnp.dot(gram_local, now, precision=HIGHEST, preferred_element_type=jnp.float32)
            now = now * top / (below + EPS)
            if it < STEPS:
                coeffs[index] = now
                numerator = numerator + dot32(now.astype(jnp.bfloat16), f)
                gram = gram + lax.dot_general(
                    now, now, NT, precision=HIGHEST, preferred_element_type=jnp.float32
                )
                return numerator, gram
            rebuilt = lax.dot_general(
                now.astype(jnp.bfloat16), basis_low, (((0,), (0,)), ((), ())),
                preferred_element_type=jnp.float32,
            ).astype(jnp.bfloat16)
            hammed = jnp.maximum(f.astype(jnp.float32) + dot32(rebuilt, w_ham[...]), 0.0)
            out[span, :] = dot32(hammed.astype(jnp.bfloat16), w_align[...]).astype(jnp.bfloat16)
            return carry

        start = (jnp.zeros((rank, channels), jnp.float32), jnp.zeros((rank, rank), jnp.float32))
        if it < STEPS:
            return lax.fori_loop(0, blocks, body, start)
        lax.fori_loop(0, blocks, lambda i, c: (body(i, start), c)[1], 0)

    basis_now[...] = bases[...]
    for it in range(STEPS):
        numerator, gram = reduce_all(it, *sums(it))
        basis = basis_now[...]
        below = jnp.dot(gram, basis, precision=HIGHEST, preferred_element_type=jnp.float32)
        basis_now[...] = basis * numerator / (below + EPS)
    sums(STEPS)
    for it in range(STEPS):
        for step in range(1, group):
            copy_a(it, step).wait_send()
            copy_c(it, step, member).wait_send()
        for step in range(1, line):
            copy_b(it, step).wait_send()


def factor(mixed, w_squeeze, bases_init, w_ham, w_align):
    n_rows, n_cols = lax.axis_size("rows"), lax.axis_size("cols")
    pair = 2 if n_cols % 2 == 0 else 1
    group, line = n_rows * pair, n_cols // pair
    pixels, channels = mixed.shape
    rank = bases_init.shape[1]
    depth, width = rank // group, channels + 2 * rank
    piece = 512 if pixels % 512 == 0 else pixels
    dma = pltpu.SemaphoreType.DMA
    vmem = pl.BlockSpec(memory_space=pltpu.VMEM)
    return pl.pallas_call(
        functools.partial(factor_kernel, (n_rows, n_cols, pair, piece)),
        out_shape=jax.ShapeDtypeStruct((pixels, channels), jnp.bfloat16),
        in_specs=[vmem] * 5,
        out_specs=vmem,
        scratch_shapes=[
            pltpu.VMEM((pixels, channels), jnp.bfloat16),
            pltpu.VMEM((pixels // piece, rank, piece), jnp.float32),
            pltpu.VMEM((rank, channels), jnp.float32),
            pltpu.VMEM((STEPS, group, depth, width), jnp.float32),
            pltpu.VMEM((STEPS, group, depth, width), jnp.float32),
            pltpu.VMEM((STEPS, depth, width), jnp.float32),
            pltpu.VMEM((STEPS, line, depth, width), jnp.float32),
            pltpu.VMEM((STEPS, group, depth, width), jnp.float32),
            dma((STEPS, group)), dma((STEPS, group)),
            dma((STEPS, line)), dma((STEPS, line)),
            dma((STEPS, group)), dma((STEPS, group)),
        ],
        compiler_params=pltpu.CompilerParams(
            collective_id=0, has_side_effects=True, vmem_limit_bytes=40 * 2**20
        ),
        cost_estimate=pl.CostEstimate(
            flops=6 * pixels * channels * channels, bytes_accessed=8 * pixels * channels,
            transcendentals=0,
        ),
    )(mixed, w_squeeze, bases_init.T, w_ham, w_align)


def on_device(band_input, column_taps, row_taps, w_squeeze, bases_init, w_ham, w_align):
    tile_rows, tile_cols, channels = band_input.shape
    margin = column_taps.shape[0] // 2
    widened = padded(band_input, (("cols", 1),), margin)
    col_filtered = filter_columns(widened, column_taps, tile_cols).astype(jnp.bfloat16)
    extended = padded(col_filtered, (("rows", 0),), margin)
    strip_sum = filter_rows(extended, row_taps, tile_rows)
    mixed_tile = (
        (band_input.astype(jnp.float32) + strip_sum)
        .astype(jnp.bfloat16)
        .reshape(tile_rows * tile_cols, channels)
    )
    head_out = factor(mixed_tile, w_squeeze, bases_init, w_ham, w_align)
    return head_out.reshape(tile_rows, tile_cols, channels)


def solution(mesh):
    in_specs = (P("rows", "cols", None), P(), P(), P(), P(), P(), P())
    out_specs = P("rows", "cols", None)
    return jax.shard_map(
        on_device, mesh=mesh, in_specs=in_specs, out_specs=out_specs, check_vma=False
    )
```

time: 484 us -> 132 us (0.27)
  waiting for transfers between devices: 271 us -> 27.2 us
  blocking collectives: 125 us -> 0 us
  Pallas kernels: 0 us -> 60.9 us
  matrix products: 30.2 us -> 0 us
  between operations: 13.5 us -> 0.23 us
    psum x3 -> x0, waiting for transfers between devices: 244 us -> none  [on_device(): numerator, gram_sum = lax.psum((numerator, gram_part), ('rows', 'cols'))]
    psum x3 -> x0, blocking collectives: 125 us -> none  [on_device(): numerator, gram_sum = lax.psum((numerator, gram_part), ('rows', 'cols'))]
    pallas_call x0 -> x1, Pallas kernels: none -> 60.9 us  [factor(): pl.pallas_call(functools.partial(factor_kernel, (n_rows, n_cols, pair, pi...]
    dot_general x24 -> x0, matrix products: 30.2 us -> none  [the longest x3 4.43 us: on_device(): lax.dot_general(feature, coeff_low, (((0,), (1,)), ((), ())), preferred_e...]
  transfers between devices with their start and end apart: 7 -> 4, of which waited for: 5 -> 2; matrix products, arithmetic and copies ran while one was open for 1% -> 1% of each run, Pallas kernels for 0% -> 0%
where the time goes in v1:
time: 132 us
  Pallas kernels  60.9 us (46%)
  other arithmetic  27.9 us (21%)
  waiting for transfers between devices  27.2 us (21%)
  starting transfers between devices  10.7 us (8%)
  local copies, waits for them, and re-layouts  5.33 us (4%)
    pallas_call x1, Pallas kernels, factor(): pl.pallas_call(functools.partial(factor_kernel, (n_rows, n_cols, pair, pi...  60.9 us
    ppermute x2, waiting for transfers between devices, padded(): before = lax.ppermute(last, axis, up)  27.2 us
    convert_element_type x1, other arithmetic, on_device(): mixed_tile = (band_input.astype(jnp.float32) + strip_sum).astype(jnp.bflo...  14.5 us
    convert_element_type x1, other arithmetic, on_device(): filter_columns(widened, column_taps, tile_cols).astype(jnp.bfloat16)  13.5 us
    ppermute x2, starting transfers between devices, padded(): before = lax.ppermute(last, axis, up)  8.07 us
  transfers between devices with their start and end apart: 4, of which 2 were waited for; matrix products, arithmetic and copies ran while one was open for 1% of the time, Pallas kernels for 0%

profile of v1, /device:TPU:0, one launch (start us, length us, event | category | flops | bytes accessed | tf_op | source)
XLA Modules:
  0.0 132.2 jit_solution(12682991106288129859)
XLA Ops:
  0.0 2.1 %fusion.41 = (bf16[64,10,512]{2,1,0:T(8,128)(2,1)S(1)}, bf16[64,10,512]{2,1,0:T(8,128)(2,1)S(1)}) fusion(bf16[64,32,512]{2,1,0:T(8,128)(2,1)} %param.7), kind=kLoop, calls=%fused_computation.98 | loop fusion | bytes 2621440 | tf_op jit(solution)/shard_map/slice | solution.py:26
  2.2 0.4 copy.12
  2.5 0.0 copy-start.5
  2.5 5.0 %collective-permute-start = (bf16[64,10,512]{2,0,1:T(8,128)(2,1)S(1)}, bf16[64,10,512]{2,0,1:T(8,128)(2,1)S(1)}, u32[]{:S(2)}, u32[]{:S(2)}) collective-permute-start(bf16[64,10,512]{2,0,1:T(8,128)(2,1)S(1)} %copy.12), channel_id=1, source_target_pairs={{0,1},{1,2},{2,3},{3,4},{4,5},{5,6},{6,7},{8,9},{9,10},{10,11},{11... | collective-permute-start | bytes 1966088 | tf_op jit(solution)/shard_map/ppermute | solution.py:27
  7.6 0.4 copy.13
  7.9 1.3 collective-permute-start.1
  9.2 0.2 constant_dynamic-update-slice_fusion
  9.5 26.0 %collective-permute-done = bf16[64,10,512]{2,0,1:T(8,128)(2,1)S(1)} collective-permute-done((bf16[64,10,512]{2,0,1:T(8,128)(2,1)S(1)}, bf16[64,10,512]{2,0,1:T(8,128)(2,1)S(1)}, u32[]{:S(2)}, u32[]{:S(2)}) %collective-permute-start) | collective-permute-done | bytes 655392 | tf_op jit(solution)/shard_map/ppermute | solution.py:27
  35.5 0.4 copy.9
  35.9 0.0 collective-permute-done.1
  35.9 0.4 copy_dynamic-update-slice_fusion
  36.3 0.0 copy-start.6
  36.4 13.5 %fusion.11 = bf16[64,32,512]{2,1,0:T(8,128)(2,1)S(1)} fusion(bf16[64,32,512]{2,1,0:T(8,128)(2,1)S(1)} %copy-done.4, bf16[64,10,512]{2,1,0:T(8,128)(2,1)S(1)} %copy.9, bf16[64,42,512]{2,1,0:T(8,128)(2,1)S(1)} %copy_dynamic-update-slice_fusion, f32[512]{0:T(512)S(1)} %bitcast.89, f32[512]{0:T(512)S(1)} %bitcast.88, f32[512]{0:T(512)S(1)} %bitcast.70, ...), kind=kLoop, calls=%fused_computation.49 | loop fusion | flops 97517568 | bytes 25864192 | tf_op jit(solution)/shard_map/convert_element_type | solution.py:231
  49.8 0.1 fusion.40
  49.9 1.3 collective-permute-start.3
  51.2 3.1 %collective-permute-start.2 = (bf16[10,32,512]{2,1,0:T(8,128)(2,1)S(1)}, bf16[10,32,512]{2,1,0:T(8,128)(2,1)S(1)}, u32[]{:S(2)}, u32[]{:S(2)}) collective-permute-start(bf16[10,32,512]{2,1,0:T(8,128)(2,1)S(1)} %get-tuple-element.5), channel_id=1, source_target_pairs={{0,8},{8,16},{16,24},{1,9},{9,17},{17,25},{2,10},{10,18},{18,26},{... | collective-permute-start | bytes 983048 | tf_op jit(solution)/shard_map/ppermute | solution.py:27
  54.3 0.0 collective-permute-done.3
  54.3 1.1 collective-permute-done.2
  55.5 14.5 %fusion.12 = bf16[64,32,512]{2,1,0:T(8,128)(2,1)S(1)} fusion(bf16[64,32,512]{2,1,0:T(8,128)(2,1)S(1)} %copy-done.4, bf16[64,32,512]{2,1,0:T(8,128)(2,1)S(1)} %fusion.11, bf16[10,32,512]{2,1,0:T(8,128)(2,1)S(1)} %collective-permute-done.3, bf16[10,32,512]{2,1,0:T(8,128)(2,1)S(1)} %collective-permute-done.2, f32[512]{0:T(512)S(1)} %bitcast.68, ...), kind=kLoop, calls=%fused_computation.50 | loop fusion | flops 89128960 | bytes 6989824 | tf_op jit(solution)/shard_map/convert_element_type | solution.py:236
  70.0 0.0 copy-done
  70.0 0.0 copy-done.1
  70.0 0.0 copy-done.2
  70.0 60.9 %shard_map.73 = bf16[2048,512]{1,0:T(8,128)(2,1)S(1)} custom-call(bf16[2048,512]{1,0:T(8,128)(2,1)S(1)} %bitcast.45, bf16[512,512]{1,0:T(8,128)(2,1)S(1)} %copy-done, f32[64,512]{1,0:T(8,128)S(1)} %bitcast.47, bf16[512,512]{1,0:T(8,128)(2,1)S(1)} %copy-done.1, bf16[512,512]{1,0:T(8,128)(2,1)S(1)} %copy-done.2), custom_call_target="tpu_custom_call" | custom-call | flops 3221225472 | bytes 8388608 | tf_op jit(solution)/shard_map/pallas_call | solution.py:199
  130.9 1.3 copy.17
  (13 shorter events, 0.1 us)
Async XLA Ops:
  0.0 9.2 %copy-start.4 = (bf16[64,32,512]{2,1,0:T(8,128)(2,1)S(1)}, bf16[64,32,512]{2,1,0:T(8,128)(2,1)}, u32[]{:S(2)}) copy-start(bf16[64,32,512]{2,1,0:T(8,128)(2,1)} %param.7) | copy-start | bytes 6291460
  2.5 6.9 %copy-start.5 = (f32[21,512]{1,0:T(8,128)S(1)}, f32[21,512]{1,0:T(8,128)}, u32[]{:S(2)}) copy-start(f32[21,512]{1,0:T(8,128)} %param.8) | copy-start | bytes 129028
  2.5 33.0 %collective-permute-start = (bf16[64,10,512]{2,0,1:T(8,128)(2,1)S(1)}, bf16[64,10,512]{2,0,1:T(8,128)(2,1)S(1)}, u32[]{:S(2)}, u32[]{:S(2)}) collective-permute-start(bf16[64,10,512]{2,0,1:T(8,128)(2,1)S(1)} %copy.12), channel_id=1, source_target_pairs={{0,1},{1,2},{2,3},{3,4},{4,5},{5,6},{6,7},{8,9},{9,10},{10,11},{11... | collective-permute-start | bytes 1966088 | tf_op jit(solution)/shard_map/ppermute | solution.py:27
  7.9 28.0 %collective-permute-start.1 = (bf16[64,10,512]{2,0,1:T(8,128)(2,1)S(1)}, bf16[64,10,512]{2,0,1:T(8,128)(2,1)S(1)}, u32[]{:S(2)}, u32[]{:S(2)}) collective-permute-start(bf16[64,10,512]{2,0,1:T(8,128)(2,1)S(1)} %copy.13), channel_id=1, source_target_pairs={{1,0},{2,1},{3,2},{4,3},{5,4},{6,5},{7,6},{9,8},{10,9},{11,10},{12... | collective-permute-start | bytes 1966088 | tf_op jit(solution)/shard_map/ppermute | solution.py:28
  36.3 17.9 %copy-start.6 = (f32[21,512]{1,0:T(8,128)S(1)}, f32[21,512]{1,0:T(8,128)}, u32[]{:S(2)}) copy-start(f32[21,512]{1,0:T(8,128)} %param.9) | copy-start | bytes 129028
  49.9 4.4 %collective-permute-start.3 = (bf16[10,32,512]{2,1,0:T(8,128)(2,1)S(1)}, bf16[10,32,512]{2,1,0:T(8,128)(2,1)S(1)}, u32[]{:S(2)}, u32[]{:S(2)}) collective-permute-start(bf16[10,32,512]{2,1,0:T(8,128)(2,1)S(1)} %get-tuple-element.6), channel_id=1, source_target_pairs={{8,0},{16,8},{24,16},{9,1},{17,9},{25,17},{10,2},{18,10},{26,18},{... | collective-permute-start | bytes 983048 | tf_op jit(solution)/shard_map/ppermute | solution.py:28
  51.2 4.3 %collective-permute-start.2 = (bf16[10,32,512]{2,1,0:T(8,128)(2,1)S(1)}, bf16[10,32,512]{2,1,0:T(8,128)(2,1)S(1)}, u32[]{:S(2)}, u32[]{:S(2)}) collective-permute-start(bf16[10,32,512]{2,1,0:T(8,128)(2,1)S(1)} %get-tuple-element.5), channel_id=1, source_target_pairs={{0,8},{8,16},{16,24},{1,9},{9,17},{17,25},{2,10},{10,18},{18,26},{... | collective-permute-start | bytes 983048 | tf_op jit(solution)/shard_map/ppermute | solution.py:27
  55.5 14.5 %copy-start = (bf16[512,512]{1,0:T(8,128)(2,1)S(1)}, bf16[512,512]{1,0:T(8,128)(2,1)}, u32[]{:S(2)}) copy-start(bf16[512,512]{1,0:T(8,128)(2,1)} %w_squeeze.1) | copy-start | bytes 1572868
  55.5 14.5 %copy-start.1 = (bf16[512,512]{1,0:T(8,128)(2,1)S(1)}, bf16[512,512]{1,0:T(8,128)(2,1)}, u32[]{:S(2)}) copy-start(bf16[512,512]{1,0:T(8,128)(2,1)} %w_ham.1) | copy-start | bytes 1572868
  55.5 14.5 %copy-start.2 = (bf16[512,512]{1,0:T(8,128)(2,1)S(1)}, bf16[512,512]{1,0:T(8,128)(2,1)}, u32[]{:S(2)}) copy-start(bf16[512,512]{1,0:T(8,128)(2,1)} %w_align.1) | copy-start | bytes 1572868
  55.5 14.5 %copy-start.3 = (f32[512,64]{0,1:T(8,128)S(1)}, f32[512,64]{0,1:T(8,128)}, u32[]{:S(2)}) copy-start(f32[512,64]{0,1:T(8,128)} %param.11) | copy-start | bytes 393220

commit v2 on v1

--- a/solution.py
+++ b/solution.py
@@ -17,43 +17,154 @@
 NT = (((1,), (1,)), ((), ()))
 
 
-def padded(x, sides, width):
-    for axis, dim in sides:
-        count, length = (lax.axis_size(axis), x.shape[dim])
-        up = [(i, (i + 1) % count) for i in range(count - 1)]
-        down = [(j, i) for i, j in up]
-        last = lax.slice_in_dim(x, length - width, length, axis=dim)
-        initial = lax.slice_in_dim(x, 0, width, axis=dim)
-        before = lax.ppermute(last, axis, up)
-        after = lax.ppermute(initial, axis, down)
-        x = jnp.concatenate([before, x, after], axis=dim)
-    return x
-
-
-def filter_columns(widened, column_taps, extent):
-    summed = jnp.zeros((widened.shape[0], extent, widened.shape[2]), jnp.float32)
-    for offset in range(column_taps.shape[0]):
-        summed = summed + column_taps[offset] * widened[:, offset : offset + extent, :].astype(
-            jnp.float32
-        )
-    return summed
-
-
-def filter_rows(extended, row_taps, extent):
-    summed = jnp.zeros((extent, extended.shape[1], extended.shape[2]), jnp.float32)
-    for offset in range(row_taps.shape[0]):
-        summed = summed + row_taps[offset] * extended[offset : offset + extent].astype(jnp.float32)
-    return summed
-
-
 def dot32(a, b):
     return jnp.dot(a, b, preferred_element_type=jnp.float32)
 
 
+def strip(load, taps, count):
+    results = [None] * count
+    for index in range(count + len(taps) - 1):
+        x = load(index).astype(jnp.float32)
+        for target in range(max(0, index - len(taps) + 1), min(count, index + 1)):
+            term = taps[index - target] * x
+            results[target] = term if results[target] is None else results[target] + term
+    return results
+
+
+def filter_strips(
+    counts, row, col, greet, band, column_taps, row_taps, mixed, wide, tall,
+    w_send, w_recv, t_send, t_recv,
+):
+    n_rows, n_cols = counts
+    tile_rows, tile_cols, channels = band.shape
+    taps = column_taps.shape[0]
+    margin = taps // 2
+    lanes = wide.shape[3]
+    blocks = channels // lanes
+    has = (
+        (col > 0, col < n_cols - 1),
+        (row > 0, row < n_rows - 1),
+    )
+
+    def edge_copy(axis, block, side):
+        buffer, length = ((wide, tile_cols), (tall, tile_rows))[axis]
+        send, recv = ((w_send, w_recv), (t_send, t_recv))[axis]
+        start = margin if side == 0 else length
+        target = margin + length if side == 0 else 0
+        step = -1 if side == 0 else 1
+        device = (row, col + step) if axis == 0 else (row + step, col)
+        return pltpu.make_async_remote_copy(
+            src_ref=buffer.at[block, pl.ds(start, margin)],
+            dst_ref=buffer.at[block, pl.ds(target, margin)],
+            send_sem=send.at[block, side], recv_sem=recv.at[block, side],
+            device_id=device, device_id_type=MESH,
+        )
+
+    def start(axis, block):
+        for side in range(2):
+            @pl.when(has[axis][side])
+            def _():
+                edge_copy(axis, block, side).start()
+
+    def wait_send(axis, block):
+        for side in range(2):
+            @pl.when(has[axis][side])
+            def _():
+                edge_copy(axis, block, side).wait_send()
+
+    def wait_recv(axis, block):
+        for side in range(2):
+            @pl.when(has[axis][1 - side])
+            def _():
+                edge_copy(axis, block, side).wait_recv()
+
+    def clear(axis):
+        buffer, length = ((wide, tile_cols), (tall, tile_rows))[axis]
+        for side, first in ((0, 0), (1, margin + length)):
+            @pl.when(jnp.logical_not(has[axis][side]))
+            def _():
+                @pl.loop(0, blocks)
+                def _(block):
+                    buffer[block, first : first + margin] = jnp.zeros(
+                        (margin,) + buffer.shape[2:], buffer.dtype
+                    )
+
+    def turn(block):
+        span = slice(block * lanes, (block + 1) * lanes)
+
+        @pl.loop(0, tile_rows // 16)
+        def _(index):
+            rows = pl.ds(pl.multiple_of(index * 16, 16), 16)
+            x = band[rows, :, span].astype(jnp.float32)
+            wide[block, margin : margin + tile_cols, rows, :] = jnp.swapaxes(x, 0, 1).astype(
+                jnp.bfloat16
+            )
+
+    def across(block):
+        span = slice(block * lanes, (block + 1) * lanes)
+        halves = tile_cols // 16
+
+        @pl.loop(0, (tile_rows // 16) * halves)
+        def _(index):
+            h = lax.div(index, halves) * 16
+            w = lax.rem(index, halves) * 16
+            rows = pl.ds(pl.multiple_of(h, 16), 16)
+            factors = [column_taps[k : k + 1, span] for k in range(taps)]
+            found = []
+            for part in range(2):
+                found += strip(
+                    lambda i: wide[block, w + part * 8 + i, rows, :], factors, 8
+                )
+            x = jnp.swapaxes(jnp.stack(found, axis=0), 0, 1).astype(jnp.bfloat16)
+            tall[block, pl.ds(margin + h, 16), pl.ds(pl.multiple_of(w, 16), 16), :] = x
+
+    def down(block):
+        span = slice(block * lanes, (block + 1) * lanes)
+        halves = tile_cols // 16
+
+        @pl.loop(0, (tile_rows // 8) * halves)
+        def _(index):
+            h = lax.div(index, halves) * 8
+            w = pl.multiple_of(lax.rem(index, halves) * 16, 16)
+            factors = [row_taps[k : k + 1, span] for k in range(taps)]
+            found = strip(lambda i: tall[block, h + i, pl.ds(w, 16), :], factors, 8)
+            for i in range(8):
+                x = band[h + i, pl.ds(w, 16), span].astype(jnp.float32) + found[i]
+                place = pl.ds(pl.multiple_of((h + i) * tile_cols + w, 16), 16)
+                mixed[place, span] = x.astype(jnp.bfloat16)
+
+    turn(0)
+    greet()
+    start(0, 0)
+    ahead = min(2, blocks)
+    for block in range(1, blocks):
+        turn(block)
+        if block < ahead:
+            start(0, block)
+    clear(0)
+    clear(1)
+    for block in range(blocks):
+        if block + ahead < blocks:
+            wait_send(0, block)
+            start(0, block + ahead)
+        wait_recv(0, block)
+        across(block)
+        start(1, block)
+        if block > 0:
+            wait_recv(1, block - 1)
+            down(block - 1)
+    wait_recv(1, blocks - 1)
+    down(blocks - 1)
+    for block in range(blocks):
+        if block + ahead >= blocks:
+            wait_send(0, block)
+        wait_send(1, block)
+
+
 def factor_kernel(
-    grid_shape, mixed, w_squeeze, bases, w_ham, w_align, out,
-    feature, coeffs, basis_now, part, arrived, line_out, line_in, gathered,
-    a_send, a_recv, b_send, b_recv, c_send, c_recv,
+    grid_shape, band, column_taps, row_taps, w_squeeze, bases, w_ham, w_align, out,
+    wide, tall, mixed, feature, coeffs, basis_now, part, arrived, line_out, line_in, gathered,
+    w_send, w_recv, t_send, t_recv, a_send, a_recv, b_send, b_recv, c_send, c_recv,
 ):
     n_rows, n_cols, pair, piece = grid_shape
     group, line = n_rows * pair, n_cols // pair
@@ -78,6 +189,21 @@
         pl.semaphore_signal(barrier, inc=1, device_id=in_group(step)[1], device_id_type=MESH)
     for step in range(1, line):
         pl.semaphore_signal(barrier, inc=1, device_id=in_line(step), device_id_type=MESH)
+    greeted = group - 1 + line - 1
+    if pair == 2:
+        outer = jnp.where(cell == 0, col - 1, col + 1)
+        has_outer = jnp.logical_and(outer >= 0, outer < n_cols)
+
+        @pl.when(has_outer)
+        def _():
+            pl.semaphore_signal(barrier, inc=1, device_id=(row, outer), device_id_type=MESH)
+
+        greeted = greeted + has_outer.astype(jnp.int32)
+
+    filter_strips(
+        (n_rows, n_cols), row, col, lambda: pl.semaphore_wait(barrier, greeted),
+        band, column_taps, row_taps, mixed, wide, tall, w_send, w_recv, t_send, t_recv,
+    )
 
     def copy_a(it, step):
         other, device = in_group(step)
@@ -105,8 +231,6 @@
         both = jnp.concatenate([numerator, gram, jnp.zeros_like(gram)], axis=1)
         for index in range(group):
             part[it, index] = both[index * depth : (index + 1) * depth]
-        if it == 0:
-            pl.semaphore_wait(barrier, group - 1 + line - 1)
         for step in range(1, group):
             copy_a(it, step).start()
         total = part[it, member]
@@ -186,22 +310,29 @@
             copy_b(it, step).wait_send()
 
 
-def factor(mixed, w_squeeze, bases_init, w_ham, w_align):
+def on_device(band_input, column_taps, row_taps, w_squeeze, bases_init, w_ham, w_align):
     n_rows, n_cols = lax.axis_size("rows"), lax.axis_size("cols")
     pair = 2 if n_cols % 2 == 0 else 1
     group, line = n_rows * pair, n_cols // pair
-    pixels, channels = mixed.shape
+    tile_rows, tile_cols, channels = band_input.shape
+    pixels = tile_rows * tile_cols
+    margin = column_taps.shape[0] // 2
     rank = bases_init.shape[1]
     depth, width = rank // group, channels + 2 * rank
     piece = 512 if pixels % 512 == 0 else pixels
+    lanes = 128
+    blocks = channels // lanes
     dma = pltpu.SemaphoreType.DMA
     vmem = pl.BlockSpec(memory_space=pltpu.VMEM)
-    return pl.pallas_call(
+    head_out = pl.pallas_call(
         functools.partial(factor_kernel, (n_rows, n_cols, pair, piece)),
         out_shape=jax.ShapeDtypeStruct((pixels, channels), jnp.bfloat16),
-        in_specs=[vmem] * 5,
+        in_specs=[vmem] * 7,
         out_specs=vmem,
         scratch_shapes=[
+            pltpu.VMEM((blocks, tile_cols + 2 * margin, tile_rows, lanes), jnp.bfloat16),
+            pltpu.VMEM((blocks, tile_rows + 2 * margin, tile_cols, lanes), jnp.bfloat16),
+            pltpu.VMEM((pixels, channels), jnp.bfloat16),
             pltpu.VMEM((pixels, channels), jnp.bfloat16),
             pltpu.VMEM((pixels // piece, rank, piece), jnp.float32),
             pltpu.VMEM((rank, channels), jnp.float32),
@@ -210,33 +341,20 @@
             pltpu.VMEM((STEPS, depth, width), jnp.float32),
             pltpu.VMEM((STEPS, line, depth, width), jnp.float32),
             pltpu.VMEM((STEPS, group, depth, width), jnp.float32),
+            dma((blocks, 2)), dma((blocks, 2)),
+            dma((blocks, 2)), dma((blocks, 2)),
             dma((STEPS, group)), dma((STEPS, group)),
             dma((STEPS, line)), dma((STEPS, line)),
             dma((STEPS, group)), dma((STEPS, group)),
         ],
         compiler_params=pltpu.CompilerParams(
-            collective_id=0, has_side_effects=True, vmem_limit_bytes=40 * 2**20
+            collective_id=0, has_side_effects=True, vmem_limit_bytes=48 * 2**20
         ),
         cost_estimate=pl.CostEstimate(
             flops=6 * pixels * channels * channels, bytes_accessed=8 * pixels * channels,
             transcendentals=0,
         ),
-    )(mixed, w_squeeze, bases_init.T, w_ham, w_align)
-
-
-def on_device(band_input, column_taps, row_taps, w_squeeze, bases_init, w_ham, w_align):
-    tile_rows, tile_cols, channels = band_input.shape
-    margin = column_taps.shape[0] // 2
-    widened = padded(band_input, (("cols", 1),), margin)
-    col_filtered = filter_columns(widened, column_taps, tile_cols).astype(jnp.bfloat16)
-    extended = padded(col_filtered, (("rows", 0),), margin)
-    strip_sum = filter_rows(extended, row_taps, tile_rows)
-    mixed_tile = (
-        (band_input.astype(jnp.float32) + strip_sum)
-        .astype(jnp.bfloat16)
-        .reshape(tile_rows * tile_cols, channels)
-    )
-    head_out = factor(mixed_tile, w_squeeze, bases_init, w_ham, w_align)
+    )(band_input, column_taps, row_taps, w_squeeze, bases_init.T, w_ham, w_align)
     return head_out.reshape(tile_rows, tile_cols, channels)
 
 

time: 132 us -> 103 us (0.78)
  Pallas kernels: 60.9 us -> 94.1 us
  other arithmetic: 27.9 us -> 0 us
  waiting for transfers between devices: 27.2 us -> 0 us
  starting transfers between devices: 10.7 us -> 0 us
  local copies, waits for them, and re-layouts: 5.33 us -> 8.53 us
    pallas_call x1, Pallas kernels: 60.9 us -> 94.1 us  [on_device(): pl.pallas_call(functools.partial(factor_kernel, (n_rows, n_cols, pair, pi...]
    convert_element_type x2 -> x0, other arithmetic: 27.9 us -> none  [the longest x1 14.5 us: on_device(): mixed_tile = (band_input.astype(jnp.float32) + strip_sum).astype(jnp.bflo...]
    ppermute x4 -> x0, waiting for transfers between devices: 27.2 us -> none  [the longest x2 27.2 us: padded(): before = lax.ppermute(last, axis, up)]
    ppermute x4 -> x0, starting transfers between devices: 10.7 us -> none  [the longest x2 8.07 us: padded(): before = lax.ppermute(last, axis, up)]
    unnamed x18 -> x15, local copies, waits for them, and re-layouts: 2.27 us -> 8.53 us
    slice x6 -> x0, local copies, waits for them, and re-layouts: 2.27 us -> none  [the longest x1 2.14 us: padded(): initial = lax.slice_in_dim(x, 0, width, axis=dim)]
  transfers between devices with their start and end apart: 4 -> 0, of which waited for: 2 -> 0; matrix products, arithmetic and copies ran while one was open for 1% -> 0% of each run, Pallas kernels for 0% -> 0%
where the time goes in v2:
time: 103 us
  Pallas kernels  94.1 us (91%)
  local copies, waits for them, and re-layouts  8.53 us (8%)
    pallas_call x1, Pallas kernels, on_device(): pl.pallas_call(functools.partial(factor_kernel, (n_rows, n_cols, pair, pi...  94.1 us
    unnamed x15, local copies, waits for them, and re-layouts  8.53 us

profile of v2, /device:TPU:0, one launch (start us, length us, event | category | flops | bytes accessed | tf_op | source)
XLA Modules:
  0.0 102.7 jit_solution(10833139195180383486)
XLA Ops:
  0.0 0.0 copy-start
  0.0 1.6 %copy-done = bf16[64,32,512]{2,1,0:T(8,128)(2,1)S(1)} copy-done((bf16[64,32,512]{2,1,0:T(8,128)(2,1)S(1)}, bf16[64,32,512]{2,1,0:T(8,128)(2,1)}, u32[]{:S(2)}) %copy-start) | copy-done | bytes 2097176
  1.6 0.0 copy-start.1
  1.6 1.0 %copy-done.1 = bf16[512,512]{1,0:T(8,128)(2,1)S(1)} copy-done((bf16[512,512]{1,0:T(8,128)(2,1)S(1)}, bf16[512,512]{1,0:T(8,128)(2,1)}, u32[]{:S(2)}) %copy-start.1) | copy-done | bytes 524312
  2.6 0.0 copy-start.2
  2.6 1.0 %copy-done.2 = bf16[512,512]{1,0:T(8,128)(2,1)S(1)} copy-done((bf16[512,512]{1,0:T(8,128)(2,1)S(1)}, bf16[512,512]{1,0:T(8,128)(2,1)}, u32[]{:S(2)}) %copy-start.2) | copy-done | bytes 524312
  3.7 0.0 copy-start.3
  3.7 1.0 %copy-done.3 = bf16[512,512]{1,0:T(8,128)(2,1)S(1)} copy-done((bf16[512,512]{1,0:T(8,128)(2,1)S(1)}, bf16[512,512]{1,0:T(8,128)(2,1)}, u32[]{:S(2)}) %copy-start.3) | copy-done | bytes 524312
  4.7 0.0 copy-start.4
  4.7 0.9 copy-done.4
  5.6 0.0 copy-start.5
  5.6 0.8 copy-done.5
  6.4 0.0 copy-start.6
  6.4 0.8 copy-done.6
  7.2 94.1 %shard_map.73 = bf16[2048,512]{1,0:T(8,128)(2,1)S(1)} custom-call(bf16[64,32,512]{2,1,0:T(8,128)(2,1)S(1)} %copy-done, f32[21,512]{1,0:T(8,128)S(1)} %copy-done.5, f32[21,512]{1,0:T(8,128)S(1)} %copy-done.6, bf16[512,512]{1,0:T(8,128)(2,1)S(1)} %copy-done.1, f32[64,512]{1,0:T(8,128)S(1)} %bitcast.3, bf16[512,512]{1,0:T(8,128)(2,1)S(1)} %copy-done.2, ...), custom_call_target="tpu_custom_call" | custom-call | flops 3221225472 | bytes 8388608 | tf_op jit(solution)/shard_map/pallas_call | solution.py:327
  101.3 1.3 %copy.9 = bf16[64,32,512]{2,1,0:T(8,128)(2,1)} copy(bf16[64,32,512]{2,1,0:T(8,128)(2,1)S(1)} %bitcast.2) | data formatting | bytes 4194304
Async XLA Ops:
  0.0 1.6 %copy-start = (bf16[64,32,512]{2,1,0:T(8,128)(2,1)S(1)}, bf16[64,32,512]{2,1,0:T(8,128)(2,1)}, u32[]{:S(2)}) copy-start(bf16[64,32,512]{2,1,0:T(8,128)(2,1)} %band.1) | copy-start | bytes 6291460
  1.6 1.0 %copy-start.1 = (bf16[512,512]{1,0:T(8,128)(2,1)S(1)}, bf16[512,512]{1,0:T(8,128)(2,1)}, u32[]{:S(2)}) copy-start(bf16[512,512]{1,0:T(8,128)(2,1)} %w_squeeze.1) | copy-start | bytes 1572868
  2.6 1.0 %copy-start.2 = (bf16[512,512]{1,0:T(8,128)(2,1)S(1)}, bf16[512,512]{1,0:T(8,128)(2,1)}, u32[]{:S(2)}) copy-start(bf16[512,512]{1,0:T(8,128)(2,1)} %w_ham.1) | copy-start | bytes 1572868
  3.7 1.0 %copy-start.3 = (bf16[512,512]{1,0:T(8,128)(2,1)S(1)}, bf16[512,512]{1,0:T(8,128)(2,1)}, u32[]{:S(2)}) copy-start(bf16[512,512]{1,0:T(8,128)(2,1)} %w_align.1) | copy-start | bytes 1572868
  4.7 0.9 copy-start.4
  5.6 0.8 copy-start.5
  6.4 0.8 copy-start.6

commit v3 on v2

--- a/solution.py
+++ b/solution.py
@@ -13,7 +13,6 @@
 EPS = 1e-06
 
 MESH = pl.DeviceIdType.MESH
-HIGHEST = lax.Precision.HIGHEST
 NT = (((1,), (1,)), ((), ()))
 
 
@@ -32,7 +31,7 @@
 
 
 def filter_strips(
-    counts, row, col, greet, band, column_taps, row_taps, mixed, wide, tall,
+    counts, row, col, greet, load_band, loads, band, column_taps, row_taps, mixed, wide, tall,
     w_send, w_recv, t_send, t_recv,
 ):
     n_rows, n_cols = counts
@@ -118,11 +117,11 @@
             x = jnp.swapaxes(jnp.stack(found, axis=0), 0, 1).astype(jnp.bfloat16)
             tall[block, pl.ds(margin + h, 16), pl.ds(pl.multiple_of(w, 16), 16), :] = x
 
-    def down(block):
+    def down(block, first, last):
         span = slice(block * lanes, (block + 1) * lanes)
         halves = tile_cols // 16
 
-        @pl.loop(0, (tile_rows // 8) * halves)
+        @pl.loop(first * halves, last * halves)
         def _(index):
             h = lax.div(index, halves) * 8
             w = pl.multiple_of(lax.rem(index, halves) * 16, 16)
@@ -133,16 +132,22 @@
                 place = pl.ds(pl.multiple_of((h + i) * tile_cols + w, 16), 16)
                 mixed[place, span] = x.astype(jnp.bfloat16)
 
+    load_band(0).wait()
     turn(0)
     greet()
     start(0, 0)
     ahead = min(2, blocks)
     for block in range(1, blocks):
+        load_band(block).wait()
         turn(block)
         if block < ahead:
             start(0, block)
     clear(0)
     clear(1)
+    for load in loads:
+        load.wait()
+    strips = tile_rows // 8
+    edge = -(-margin // 8)
     for block in range(blocks):
         if block + ahead < blocks:
             wait_send(0, block)
@@ -150,28 +155,68 @@
         wait_recv(0, block)
         across(block)
         start(1, block)
-        if block > 0:
-            wait_recv(1, block - 1)
-            down(block - 1)
-    wait_recv(1, blocks - 1)
-    down(blocks - 1)
+        down(block, edge, strips - edge)
+        wait_recv(1, block)
+        down(block, 0, edge)
+        down(block, strips - edge, strips)
     for block in range(blocks):
         if block + ahead >= blocks:
             wait_send(0, block)
         wait_send(1, block)
 
 
+def split(x):
+    high = x.astype(jnp.bfloat16)
+    return high, (x - high.astype(jnp.float32)).astype(jnp.bfloat16)
+
+
+def product(a, b):
+    a_high, a_low = split(a)
+    b_high, b_low = split(b)
+    return dot32(
+        jnp.concatenate([a_high, a_low, a_high], axis=1),
+        jnp.concatenate([b_high, b_high, b_low], axis=0),
+    )
+
+
+def gram_of(stacked):
+    n = stacked.shape[0] // 2
+    both = lax.dot_general(stacked, stacked, NT, preferred_element_type=jnp.float32)
+    return both[:n, :n] + (both[:n, n:] + both[n:, :n])
+
+
 def factor_kernel(
-    grid_shape, band, column_taps, row_taps, w_squeeze, bases, w_ham, w_align, out,
-    wide, tall, mixed, feature, coeffs, basis_now, part, arrived, line_out, line_in, gathered,
+    grid_shape, *refs,
+):
+    sources, out = refs[:7], refs[7]
+    band, column_taps, row_taps, w_squeeze, basis_now, w_ham, w_align = refs[8:15]
+    (
+    wide, tall, mixed, feature, coeffs, halves, part, arrived, line_out, line_in, gathered,
     w_send, w_recv, t_send, t_recv, a_send, a_recv, b_send, b_recv, c_send, c_recv,
-):
+    load_sem, band_sem, out_sem,
+    ) = refs[15:]
     n_rows, n_cols, pair, piece = grid_shape
     group, line = n_rows * pair, n_cols // pair
     pixels, channels = mixed.shape
-    rank = bases.shape[0]
+    rank = basis_now.shape[0]
     depth = rank // group
     blocks = pixels // piece
+
+    lanes = wide.shape[3]
+
+    def load_band(block):
+        span = slice(block * lanes, (block + 1) * lanes)
+        return pltpu.make_async_copy(
+            sources[0].at[:, :, span], band.at[:, :, span], band_sem.at[block]
+        )
+
+    loads = [
+        pltpu.make_async_copy(sources[i], refs[8 + i], load_sem.at[i]) for i in range(1, 7)
+    ]
+    for block in range(channels // lanes):
+        load_band(block).start()
+    for load in loads:
+        load.start()
 
     row, col = lax.axis_index("rows"), lax.axis_index("cols")
     cell, along = lax.rem(col, pair), lax.div(col, pair)
@@ -202,7 +247,7 @@
 
     filter_strips(
         (n_rows, n_cols), row, col, lambda: pl.semaphore_wait(barrier, greeted),
-        band, column_taps, row_taps, mixed, wide, tall, w_send, w_recv, t_send, t_recv,
+        load_band, loads, band, column_taps, row_taps, mixed, wide, tall, w_send, w_recv, t_send, t_recv,
     )
 
     def copy_a(it, step):
@@ -252,62 +297,72 @@
         whole = jnp.concatenate([gathered[it, index] for index in range(group)], axis=0)
         return whole[:, :channels], whole[:, channels : channels + rank]
 
+    def squeeze():
+        @pl.loop(0, blocks)
+        def _(index):
+            span = pl.ds(pl.multiple_of(index * piece, piece), piece)
+            feature[span, :] = jnp.maximum(dot32(mixed[span, :], w_squeeze[...]), 0.0).astype(
+                jnp.bfloat16
+            )
+
     def sums(it):
         basis = basis_now[...]
         basis_low = basis.astype(jnp.bfloat16)
-        gram_local = lax.dot_general(
-            basis, basis, NT, precision=HIGHEST, preferred_element_type=jnp.float32
-        )
-
-        def body(index, carry):
-            numerator, gram = carry
-            span = pl.ds(pl.multiple_of(index * piece, piece), piece)
-            if it == 0:
-                f = jnp.maximum(dot32(mixed[span, :], w_squeeze[...]), 0.0).astype(jnp.bfloat16)
-                feature[span, :] = f
-            else:
-                f = feature[span, :]
-            top = lax.dot_general(basis_low, f, NT, preferred_element_type=jnp.float32)
+        gram_local = gram_of(jnp.concatenate(split(basis), axis=0))
+        for index in range(blocks):
+            span = slice(index * piece, (index + 1) * piece)
+            top = lax.dot_general(
+                basis_low, feature[span, :], NT, preferred_element_type=jnp.float32
+            )
             if it == 0:
                 weight = jnp.exp(top - jnp.max(top, axis=0, keepdims=True))
                 now = weight / jnp.sum(weight, axis=0, keepdims=True)
             else:
-                now = coeffs[index]
-            below = jnp.dot(gram_local, now, precision=HIGHEST, preferred_element_type=jnp.float32)
-            now = now * top / (below + EPS)
-            if it < STEPS:
-                coeffs[index] = now
-                numerator = numerator + dot32(now.astype(jnp.bfloat16), f)
-                gram = gram + lax.dot_general(
-                    now, now, NT, precision=HIGHEST, preferred_element_type=jnp.float32
-                )
-                return numerator, gram
+                now = coeffs[:, span]
+            now = now * top / (product(gram_local, now) + EPS)
+            coeffs[:, span] = now
+            high, low = split(now)
+            halves[:rank, span] = high
+            halves[rank:, span] = low
+        stacked = halves[...]
+        return dot32(stacked[:rank], feature[...]), gram_of(stacked)
+
+    def finish():
+        basis = basis_now[...]
+        basis_low = basis.astype(jnp.bfloat16)
+        gram_local = gram_of(jnp.concatenate(split(basis), axis=0))
+        for index in range(blocks):
+            span = slice(index * piece, (index + 1) * piece)
+            f = feature[span, :]
+            top = lax.dot_general(basis_low, f, NT, preferred_element_type=jnp.float32)
+            now = coeffs[:, span]
+            now = now * top / (product(gram_local, now) + EPS)
             rebuilt = lax.dot_general(
                 now.astype(jnp.bfloat16), basis_low, (((0,), (0,)), ((), ())),
                 preferred_element_type=jnp.float32,
             ).astype(jnp.bfloat16)
             hammed = jnp.maximum(f.astype(jnp.float32) + dot32(rebuilt, w_ham[...]), 0.0)
-            out[span, :] = dot32(hammed.astype(jnp.bfloat16), w_align[...]).astype(jnp.bfloat16)
-            return carry
-
-        start = (jnp.zeros((rank, channels), jnp.float32), jnp.zeros((rank, rank), jnp.float32))
-        if it < STEPS:
-            return lax.fori_loop(0, blocks, body, start)
-        lax.fori_loop(0, blocks, lambda i, c: (body(i, start), c)[1], 0)
-
-    basis_now[...] = bases[...]
+            mixed[span, :] = dot32(hammed.astype(jnp.bfloat16), w_align[...]).astype(jnp.bfloat16)
+            store(index).start()
+
+    def store(index):
+        span = slice(index * piece, (index + 1) * piece)
+        return pltpu.make_async_copy(mixed.at[span], out.at[span], out_sem.at[index])
+
+    squeeze()
     for it in range(STEPS):
         numerator, gram = reduce_all(it, *sums(it))
         basis = basis_now[...]
-        below = jnp.dot(gram, basis, precision=HIGHEST, preferred_element_type=jnp.float32)
-        basis_now[...] = basis * numerator / (below + EPS)
-    sums(STEPS)
+        basis_now[...] = basis * numerator / (product(gram, basis) + EPS)
+    finish()
     for it in range(STEPS):
         for step in range(1, group):
             copy_a(it, step).wait_send()
             copy_c(it, step, member).wait_send()
         for step in range(1, line):
             copy_b(it, step).wait_send()
+    for index in range(blocks):
+        store(index).wait()
 
 
 def on_device(band_input, column_taps, row_taps, w_squeeze, bases_init, w_ham, w_align):
@@ -323,19 +378,19 @@
     lanes = 128
     blocks = channels // lanes
     dma = pltpu.SemaphoreType.DMA
-    vmem = pl.BlockSpec(memory_space=pltpu.VMEM)
+    operands = (band_input, column_taps, row_taps, w_squeeze, bases_init.T, w_ham, w_align)
     head_out = pl.pallas_call(
         functools.partial(factor_kernel, (n_rows, n_cols, pair, piece)),
         out_shape=jax.ShapeDtypeStruct((pixels, channels), jnp.bfloat16),
-        in_specs=[vmem] * 7,
-        out_specs=vmem,
-        scratch_shapes=[
+        in_specs=[pl.BlockSpec(memory_space=pltpu.HBM)] * 7,
+        out_specs=pl.BlockSpec(memory_space=pltpu.HBM),
+        scratch_shapes=[pltpu.VMEM(x.shape, x.dtype) for x in operands] + [
             pltpu.VMEM((blocks, tile_cols + 2 * margin, tile_rows, lanes), jnp.bfloat16),
             pltpu.VMEM((blocks, tile_rows + 2 * margin, tile_cols, lanes), jnp.bfloat16),
             pltpu.VMEM((pixels, channels), jnp.bfloat16),
             pltpu.VMEM((pixels, channels), jnp.bfloat16),
-            pltpu.VMEM((pixels // piece, rank, piece), jnp.float32),
-            pltpu.VMEM((rank, channels), jnp.float32),
+            pltpu.VMEM((rank, pixels), jnp.float32),
+            pltpu.VMEM((2 * rank, pixels), jnp.bfloat16),
             pltpu.VMEM((STEPS, group, depth, width), jnp.float32),
             pltpu.VMEM((STEPS, group, depth, width), jnp.float32),
             pltpu.VMEM((STEPS, depth, width), jnp.float32),
@@ -346,6 +401,7 @@
             dma((STEPS, group)), dma((STEPS, group)),
             dma((STEPS, line)), dma((STEPS, line)),
             dma((STEPS, group)), dma((STEPS, group)),
+            dma((7,)), dma((blocks,)), dma((pixels // piece,)),
         ],
         compiler_params=pltpu.CompilerParams(
             collective_id=0, has_side_effects=True, vmem_limit_bytes=48 * 2**20
@@ -354,7 +410,7 @@
             flops=6 * pixels * channels * channels, bytes_accessed=8 * pixels * channels,
             transcendentals=0,
         ),
-    )(band_input, column_taps, row_taps, w_squeeze, bases_init.T, w_ham, w_align)
+    )(*operands)
     return head_out.reshape(tile_rows, tile_cols, channels)
 
 

time: 103 us -> 104 us (level)
  no operation moved by 1% of the time
where the time goes in v3:
time: 104 us; the launch traced here: 103 us
  Pallas kernels  94.6 us (91%)
  local copies, waits for them, and re-layouts  8.53 us (8%)
    pallas_call x1, Pallas kernels, on_device(): pl.pallas_call(functools.partial(factor_kernel, (n_rows, n_cols, pair, pi...  94.6 us
    unnamed x15, local copies, waits for them, and re-layouts  8.53 us

profile of v3, /device:TPU:0, one launch (start us, length us, event | category | flops | bytes accessed | tf_op | source)
XLA Modules:
  0.0 103.2 jit_solution(3269778365293017091)
XLA Ops:
  0.0 0.0 copy-start
  0.0 1.6 %copy-done = bf16[64,32,512]{2,1,0:T(8,128)(2,1)S(1)} copy-done((bf16[64,32,512]{2,1,0:T(8,128)(2,1)S(1)}, bf16[64,32,512]{2,1,0:T(8,128)(2,1)}, u32[]{:S(2)}) %copy-start) | copy-done | bytes 2097176
  1.6 0.0 copy-start.1
  1.6 1.0 %copy-done.1 = bf16[512,512]{1,0:T(8,128)(2,1)S(1)} copy-done((bf16[512,512]{1,0:T(8,128)(2,1)S(1)}, bf16[512,512]{1,0:T(8,128)(2,1)}, u32[]{:S(2)}) %copy-start.1) | copy-done | bytes 524312
  2.6 0.0 copy-start.2
  2.6 1.0 %copy-done.2 = bf16[512,512]{1,0:T(8,128)(2,1)S(1)} copy-done((bf16[512,512]{1,0:T(8,128)(2,1)S(1)}, bf16[512,512]{1,0:T(8,128)(2,1)}, u32[]{:S(2)}) %copy-start.2) | copy-done | bytes 524312
  3.7 0.0 copy-start.3
  3.7 1.0 %copy-done.3 = bf16[512,512]{1,0:T(8,128)(2,1)S(1)} copy-done((bf16[512,512]{1,0:T(8,128)(2,1)S(1)}, bf16[512,512]{1,0:T(8,128)(2,1)}, u32[]{:S(2)}) %copy-start.3) | copy-done | bytes 524312
  4.7 0.0 copy-start.4
  4.7 0.9 copy-done.4
  5.6 0.0 copy-start.5
  5.6 0.8 copy-done.5
  6.4 0.0 copy-start.6
  6.4 0.8 copy-done.6
  7.2 94.6 %shard_map.73 = bf16[2048,512]{1,0:T(8,128)(2,1)S(1)} custom-call(bf16[64,32,512]{2,1,0:T(8,128)(2,1)S(1)} %copy-done, f32[21,512]{1,0:T(8,128)S(1)} %copy-done.5, f32[21,512]{1,0:T(8,128)S(1)} %copy-done.6, bf16[512,512]{1,0:T(8,128)(2,1)S(1)} %copy-done.1, f32[64,512]{1,0:T(8,128)S(1)} %bitcast.3, bf16[512,512]{1,0:T(8,128)(2,1)S(1)} %copy-done.2, ...), custom_call_target="tpu_custom_call" | custom-call | flops 3221225472 | bytes 8388608 | tf_op jit(solution)/shard_map/pallas_call | solution.py:382
  101.9 1.3 %copy.9 = bf16[64,32,512]{2,1,0:T(8,128)(2,1)} copy(bf16[64,32,512]{2,1,0:T(8,128)(2,1)S(1)} %bitcast.2) | data formatting | bytes 4194304
Async XLA Ops:
  0.0 1.6 %copy-start = (bf16[64,32,512]{2,1,0:T(8,128)(2,1)S(1)}, bf16[64,32,512]{2,1,0:T(8,128)(2,1)}, u32[]{:S(2)}) copy-start(bf16[64,32,512]{2,1,0:T(8,128)(2,1)} %refs_0_.1) | copy-start | bytes 6291460
  1.6 1.0 %copy-start.1 = (bf16[512,512]{1,0:T(8,128)(2,1)S(1)}, bf16[512,512]{1,0:T(8,128)(2,1)}, u32[]{:S(2)}) copy-start(bf16[512,512]{1,0:T(8,128)(2,1)} %refs_3_.1) | copy-start | bytes 1572868
  2.6 1.0 %copy-start.2 = (bf16[512,512]{1,0:T(8,128)(2,1)S(1)}, bf16[512,512]{1,0:T(8,128)(2,1)}, u32[]{:S(2)}) copy-start(bf16[512,512]{1,0:T(8,128)(2,1)} %refs_5_.1) | copy-start | bytes 1572868
  3.7 1.0 %copy-start.3 = (bf16[512,512]{1,0:T(8,128)(2,1)S(1)}, bf16[512,512]{1,0:T(8,128)(2,1)}, u32[]{:S(2)}) copy-start(bf16[512,512]{1,0:T(8,128)(2,1)} %refs_6_.1) | copy-start | bytes 1572868
  4.7 0.9 copy-start.4
  5.6 0.8 copy-start.5
  6.4 0.8 copy-start.6

commit v4 on v3

--- a/solution.py
+++ b/solution.py
@@ -404,7 +404,7 @@
             dma((7,)), dma((blocks,)), dma((pixels // piece,)),
         ],
         compiler_params=pltpu.CompilerParams(
-            collective_id=0, has_side_effects=True, vmem_limit_bytes=48 * 2**20
+            collective_id=0, has_side_effects=True, vmem_limit_bytes=63 * 2**20
         ),
         cost_estimate=pl.CostEstimate(
             flops=6 * pixels * channels * channels, bytes_accessed=8 * pixels * channels,

time: 104 us -> 97.1 us (0.934)
  local copies, waits for them, and re-layouts: 8.53 us -> 3.16 us
    unnamed x15 -> x1, local copies, waits for them, and re-layouts: 8.53 us -> 3.16 us
where the time goes in v4:
time: 97.1 us; the launch traced here: 97 us
  Pallas kernels  93.8 us (97%)
  local copies, waits for them, and re-layouts  3.16 us (3%)
    pallas_call x1, Pallas kernels, on_device(): pl.pallas_call(functools.partial(factor_kernel, (n_rows, n_cols, pair, pi...  93.8 us
    unnamed x1, local copies, waits for them, and re-layouts  3.16 us

profile of v4, /device:TPU:0, one launch (start us, length us, event | category | flops | bytes accessed | tf_op | source)
XLA Modules:
  0.0 97.0 jit_solution(5647926491278290498)
XLA Ops:
  0.0 93.8 %shard_map.73 = bf16[2048,512]{1,0:T(8,128)(2,1)} custom-call(bf16[64,32,512]{2,1,0:T(8,128)(2,1)} %refs_0_.1, f32[21,512]{1,0:T(8,128)} %refs_1_.1, f32[21,512]{1,0:T(8,128)} %refs_2_.1, bf16[512,512]{1,0:T(8,128)(2,1)} %refs_3_.1, f32[64,512]{1,0:T(8,128)} %bitcast.3, bf16[512,512]{1,0:T(8,128)(2,1)} %refs_5_.1, bf16[512,512]{1,0:T(8,128)(2,1)} %refs_6_.1), custom_call_target="tpu_custom_call" | custom-call | flops 3221225472 | bytes 8388608 | tf_op jit(solution)/shard_map/pallas_call | solution.py:382
  93.8 3.2 %copy.9 = bf16[64,32,512]{2,1,0:T(8,128)(2,1)} copy(bf16[64,32,512]{2,1,0:T(8,128)(2,1)} %bitcast.2) | data formatting | bytes 4194304
